TPU v7x, 256 devices: a whole 4x4x8 slice. The times are simulated.
256 devices in a mesh: row: 8 (over x, y_lo), col: 32 (over y_hi, z, core).
Axes of the slice: x: 4, y: 4 (y_hi: 2, y_lo: 2; y = y_hi * 2 + y_lo), z: 8, core: 2. Of those that a mesh axis runs over, the one named last changes fastest.
Arguments:
- theta_hat: float32 [256, 2, 256, 512], P('row', None, 'col'), may hold values from -6 to 6
- velocity: float32 [3, 256, 512, 512], P(None, 'row', 'col'), may hold values from -6 to 6
- wall_derivative: float32 [512, 512], replicated, may hold values from -0.25 to 0.25
- to_basis: float32 [512, 512], replicated, may hold values from -0.25 to 0.25
- from_basis: float32 [512, 512], replicated, may hold values from -0.25 to 0.25
- eigenvalues: float32 [512], replicated, may hold values from 0.05 to 20
Outputs:
- theta_next: float32 [256, 2, 256, 512], P('row', None, 'col')
All inputs are finite; a program needn't handle non-finite values.
Results may differ from a plain program's by a relative error of at most 0.00005.
Values sent between devices are 32-bit elements; how exact they have to be, the bound alone decides.
A program may use at most 128 MiB of HBM per device.

v0:
```python
import math

import jax
import jax.numpy as jnp
import ml_dtypes
import numpy as np
from jax import lax
from jax.experimental import pallas as pl
from jax.experimental.pallas import tpu as pltpu
from jax.sharding import PartitionSpec as P

NX = 512
NY = 512
NZ = 256
KX = 256
WAVE_ALONG = 0.01
WAVE_SPAN = 0.02
TIME_STEP = 0.25
DIFFUSIVITY = 2.0

F32 = jnp.float32
BF16 = jnp.bfloat16
MESH = pl.DeviceIdType.MESH
VMEM_LIMIT = 60 * 1024 * 1024


def split_table(table):
    table = table.astype(np.float32)
    high = table.astype(ml_dtypes.bfloat16)
    low = (table - high.astype(np.float32)).astype(ml_dtypes.bfloat16)
    return np.stack([high, low])


def span_tables():
    z = np.arange(NZ).reshape(4, 1, 64, 1, 1, 1)
    d = np.arange(2).reshape(1, 2, 1, 1, 1, 1)
    c = np.arange(2).reshape(1, 1, 1, 2, 1, 1)
    q = np.arange(NZ).reshape(32, 8).T.reshape(1, 1, 1, 1, 8, 32)
    angle = 2.0 * math.pi * ((z * q) % NZ) / NZ
    signed = WAVE_SPAN * np.where(q < NZ // 2, q, q - NZ)
    factor = 1.0 / math.sqrt(NZ)
    inverse = factor * np.cos(angle + 0.5 * math.pi * (c - d))
    derive = factor * signed * np.cos(angle + 0.5 * math.pi * (c + 1 - d))
    q = np.arange(NZ).reshape(32, 1, 8, 1, 1, 1)
    d = np.arange(2).reshape(1, 2, 1, 1, 1, 1)
    z = np.arange(NZ).reshape(1, 1, 1, 4, 1, 64)
    c = np.arange(2).reshape(1, 1, 1, 1, 2, 1)
    angle = -2.0 * math.pi * ((z * q) % NZ) / NZ
    forward = -TIME_STEP * factor * np.cos(angle + 0.5 * math.pi * (c - d))
    return [split_table(t.reshape(512, 512)) for t in (inverse, derive, forward)]


def along_tables():
    p = np.arange(KX).reshape(4, 2, 1, 32, 1)
    d = np.arange(2).reshape(1, 1, 2, 1, 1)
    x = np.arange(NX).reshape(1, 1, 1, 1, NX)
    angle = 2.0 * math.pi * ((p * x) % NX) / NX
    factor = math.sqrt(2.0 / NX)
    inverse = (factor * np.cos(angle + 0.5 * math.pi * d)).reshape(512, 512)
    derive = (factor * WAVE_ALONG * p * np.cos(angle + 0.5 * math.pi * (d + 1))).reshape(512, 512)
    return [split_table(t) for t in (inverse, derive, inverse.T)]


def split(value):
    high = value.astype(BF16)
    return high, (value - high.astype(F32)).astype(BF16)


def dot3(a, b, dims=(((1,), (0,)), ((), ()))):
    def one(u, v):
        return lax.dot_general(u, v, dims, preferred_element_type=F32)

    return one(a[0], b[0]) + (one(a[0], b[1]) + one(a[1], b[0]))


def regroup(v):
    lane = lax.broadcasted_iota(jnp.int32, v[0].shape, 1)
    low = lane < 64
    odd = (lane // 32) % 2 == 1
    a0 = jnp.where(low, v[0], pltpu.roll(v[2], 64, 1))
    a2 = jnp.where(low, pltpu.roll(v[0], 64, 1), v[2])
    a1 = jnp.where(low, v[1], pltpu.roll(v[3], 64, 1))
    a3 = jnp.where(low, pltpu.roll(v[1], 64, 1), v[3])
    return (
        jnp.where(odd, pltpu.roll(a1, 32, 1), a0),
        jnp.where(odd, a1, pltpu.roll(a0, 96, 1)),
        jnp.where(odd, pltpu.roll(a3, 32, 1), a2),
        jnp.where(odd, a3, pltpu.roll(a2, 96, 1)),
    )


def wrap(value, n):
    return jnp.where(value >= n, value - n, value)


def kernel(
    theta, velocity, wall, to_basis, from_basis, eig,
    span_inv_h, span_der_h, span_fwd_h, along_inv_h, along_der_h, along_fwd_h,
    out,
    th_v, t0, mat_v, tb_v, fb_v, eig_v, vel_v,
    span_inv, span_der, span_fwd, along_inv, along_der, along_fwd,
    d_hl, t_hl, tb_hl, fb_hl, inv_div,
    fs, fr, x_hl, xs, xr, y_hl, adv_hl, xbs, xbr, l_hl, bs, br, c_hl, ov,
    load_sem, vel_send, vel_recv, f_send, f_recv, x_send, x_recv, xb_send, xb_recv, b_send, b_recv, out_sem,
):
    row = lax.axis_index("row")
    col = lax.axis_index("col")
    mx = row // 2
    ml = row % 2
    me = col * 2 + ml

    loads = [
        pltpu.make_async_copy(s, d, load_sem.at[i])
        for i, (s, d) in enumerate(
            [
                (wall, mat_v), (span_inv_h, span_inv), (span_der_h, span_der),
                (along_inv_h, along_inv), (along_der_h, along_der), (along_fwd_h, along_fwd),
                (span_fwd_h, span_fwd), (to_basis, tb_v), (from_basis, fb_v), (eig, eig_v),
            ]
        )
    ]
    first = [
        pltpu.make_async_copy(theta.at[:, pl.ds(b * 128, 128)], th_v.at[b], load_sem.at[10 + b]) for b in range(4)
    ]
    own_vel = [
        pltpu.make_async_copy(
            velocity.at[:, :, pl.ds(pl.multiple_of(ml * 8, 8), 8), pl.ds(b * 128, 128)],
            vel_v.at[:, b, pl.ds(ml * 32, 32)],
            load_sem.at[14 + b],
        )
        for b in range(4)
    ]
    for copy in first + loads + own_vel:
        copy.start()

    barrier = pltpu.get_barrier_semaphore()

    def partner(k):
        other = wrap(me + k, 64)
        return other, {"row": mx * 2 + other % 2, "col": other // 2}

    def greet(k, carry):
        pl.semaphore_signal(barrier, inc=1, device_id=partner(k)[1], device_id_type=MESH)
        return carry

    lax.fori_loop(1, 64, greet, 0)
    for k in range(1, 4):
        pl.semaphore_signal(
            barrier, inc=1, device_id={"row": wrap(mx + k, 4) * 2 + ml, "col": col}, device_id_type=MESH
        )

    for b in range(4):
        first[b].wait()
        for g in range(4):
            block = jnp.concatenate([th_v[b, pl.ds(4 * g + i, 32, stride=16), :] for i in range(4)], axis=0)
            t0[g, pl.ds(b * 128, 128), :] = block.T

    sub = lax.broadcasted_iota(jnp.int32, (16, 8, 128), 1) < 4

    def blocks(f, i, value):
        value = [v.reshape(16, 8, 128) for v in value]
        rows = pl.ds(pl.multiple_of(i * 16, 16), 16)
        for g in range(2):
            left, right = value[g], value[2 + g]
            fs[f, 0, rows, pl.ds(g * 8, 8), :] = jnp.where(sub, left, pltpu.roll(right, 4, 1))
            fs[f, 1, rows, pl.ds(g * 8, 8), :] = jnp.where(sub, pltpu.roll(left, 4, 1), right)

    def theta_blocks(i, carry):
        rows = pl.ds(pl.multiple_of(i * 128, 128), 128)
        value = [t0[g, rows, :] for g in range(4)]
        blocks(0, i, value)
        for g in range(4):
            lanes = pl.ds(g * 128, 128)
            t_hl[0, rows, lanes], t_hl[1, rows, lanes] = split(value[g])
        return carry

    lax.fori_loop(0, 4, theta_blocks, 0)

    pl.semaphore_wait(barrier, 66)

    def send_fwd(f, c, velocity_too):
        mine = pl.ds(pl.multiple_of(me * 16, 16), 16)
        pltpu.make_async_copy(fs.at[f, c, me], fr.at[f, c, mine], f_recv.at[f, c]).start()

        def one(k, carry):
            other, device = partner(k)
            pltpu.make_async_remote_copy(
                src_ref=fs.at[f, c, other],
                dst_ref=fr.at[f, c, mine],
                send_sem=f_send.at[f, c],
                recv_sem=f_recv.at[f, c],
                device_id=device,
                device_id_type=MESH,
            ).start()
            return carry

        def piece(i, carry):
            lax.fori_loop(1 + 4 * i, jnp.minimum(5 + 4 * i, 64), one, 0)
            send_vel(i)
            return carry

        if velocity_too:
            lax.fori_loop(0, 16, piece, 0)
        else:
            lax.fori_loop(1, 64, one, 0)

    def send_vel(i):
        pltpu.make_async_remote_copy(
            src_ref=velocity.at[
                :,
                pl.ds(i % 4 * 8, 8),
                pl.ds(pl.multiple_of((1 - ml) * 8, 8), 8),
                pl.ds(pl.multiple_of(i // 4 * 128, 128), 128),
            ],
            dst_ref=vel_v.at[:, i // 4, pl.ds(ml * 32 + i % 4 * 8, 8)],
            send_sem=vel_send,
            recv_sem=vel_recv,
            device_id={"row": mx * 2 + 1 - ml, "col": col},
            device_id_type=MESH,
        ).start()

    send_fwd(0, 0, False)

    loads[0].wait()

    def slope(i, carry):
        r = pl.multiple_of(i * 128, 128)
        value = dot3(split(mat_v[pl.ds(r, 128), :]), (t_hl[0], t_hl[1]))
        blocks(1, i, [value[:, g * 128 : g * 128 + 128] for g in range(4)])
        return carry

    lax.fori_loop(0, 4, slope, 0)
    send_fwd(1, 0, False)
    send_fwd(0, 1, True)
    send_fwd(1, 1, False)

    for copy in loads[1:]:
        copy.wait()

    def halves(i, carry):
        r = pl.multiple_of(i * 64, 64)
        tb_hl[0, pl.ds(r, 64), :], tb_hl[1, pl.ds(r, 64), :] = split(tb_v[pl.ds(r, 64), :])
        fb_hl[0, pl.ds(r, 64), :], fb_hl[1, pl.ds(r, 64), :] = split(fb_v[pl.ds(r, 64), :])
        return carry

    lax.fori_loop(0, 8, halves, 0)
    lane = lax.broadcasted_iota(jnp.int32, (1, 512), 1)
    along_wave = WAVE_ALONG * (row * 32 + lane % 32).astype(F32)
    span_id = col * 8 + (lane // 32) % 8
    span_wave = WAVE_SPAN * jnp.where(span_id < NZ // 2, span_id, span_id - NZ).astype(F32)
    waves = along_wave * along_wave + span_wave * span_wave
    for kb in range(4):
        column = jnp.broadcast_to(eig_v[:, pl.ds(kb * 128, 128)], (128, 128)).T
        for g in range(4):
            total = waves[:, g * 128 : g * 128 + 128] + column
            inv_div[pl.ds(kb * 128, 128), pl.ds(g * 128, 128)] = 1.0 / (1.0 + TIME_STEP * DIFFUSIVITY * total)
    for copy in own_vel:
        copy.wait()

    def wait_all(ref, sem):
        pltpu.make_async_copy(ref, ref, sem).wait()

    def span_stage(f, c):
        wait_all(fr.at[f, c], f_recv.at[f, c])
        for yl in range(2):
            for qh in range(2):
                for g in range(2):
                    v = [
                        fr[f, c, pl.ds(yl * 16 + g * 8 + qh * 4 + j, 32, stride=32), :] for j in range(4)
                    ]
                    for i, u in enumerate(regroup(v)):
                        r = (qh * 8 + g * 4 + i) * 32
                        x_hl[0, pl.ds(r, 32), pl.ds(yl * 128, 128)], x_hl[1, pl.ds(r, 32), pl.ds(yl * 128, 128)] = split(u)

        def lift(table, h):
            def one(k, carry):
                other = wrap(mx + k, 4)
                r = pl.multiple_of(other * 128, 128)
                xs[c, h, pl.ds(r, 128), :] = dot3(
                    (table[0, pl.ds(r, 128), :], table[1, pl.ds(r, 128), :]), (x_hl[0], x_hl[1])
                )
                pltpu.make_async_remote_copy(
                    src_ref=xs.at[c, h, pl.ds(r, 128)],
                    dst_ref=xr.at[c, h, pl.ds(pl.multiple_of(mx * 128, 128), 128)],
                    send_sem=x_send.at[c, h],
                    recv_sem=x_recv.at[c, h],
                    device_id={"row": other * 2 + ml, "col": col},
                    device_id_type=MESH,
                ).start()
                return carry

            lax.fori_loop(1, 4, one, 0)
            r = pl.multiple_of(mx * 128, 128)
            xs[c, h, pl.ds(r, 128), :] = dot3(
                (table[0, pl.ds(r, 128), :], table[1, pl.ds(r, 128), :]), (x_hl[0], x_hl[1])
            )
            pltpu.make_async_copy(xs.at[c, h, pl.ds(r, 128)], xr.at[c, h, pl.ds(r, 128)], x_recv.at[c, h]).start()

        if f == 0:
            lift(span_inv, 0)
            lift(span_der, 1)
        else:
            lift(span_inv, 2)

    def gather_lines(c, h):
        wait_all(xr.at[c, h], x_recv.at[c, h])

        def one(x, carry):
            r = pl.multiple_of(x * 128, 128)
            v = [xr[c, h, pl.ds(r + d * 64, 64), pl.ds(yl * 128, 128)] for yl in range(2) for d in range(2)]
            for j, u in enumerate(regroup(v)):
                lanes = pl.ds(r, 128)
                y_hl[h, 0, pl.ds(j * 64, 64), lanes], y_hl[h, 1, pl.ds(j * 64, 64), lanes] = split(u)
            return carry

        lax.fori_loop(0, 4, one, 0)

    def along_stage(c):
        flat = vel_v.reshape(3, 4, 512, 128)
        for h in range(3):
            gather_lines(c, h)

        def one(n, carry):
            lanes = pl.ds(pl.multiple_of(n * 256, 256), 256)
            total = None
            for h, (table, component) in enumerate(((along_der, 0), (along_inv, 2), (along_inv, 1))):
                grad = dot3((y_hl[h, 0], y_hl[h, 1]), (table[0, :, lanes], table[1, :, lanes]))
                speed = jnp.concatenate(
                    [
                        jnp.concatenate(
                            [flat[component, 2 * n + b, pl.ds(4 * c + j, 64, stride=8), :] for j in range(4)], axis=0
                        )
                        for b in range(2)
                    ],
                    axis=1,
                )
                term = grad * speed
                total = term if total is None else total + term
            adv_hl[0, :, lanes], adv_hl[1, :, lanes] = split(total)
            return carry

        lax.fori_loop(0, 2, one, 0)

        def back(k, carry):
            other = wrap(mx + k, 4)
            r = pl.multiple_of(other * 128, 128)
            lanes = pl.ds(r, 128)
            modes = dot3((adv_hl[0], adv_hl[1]), (along_fwd[0, :, lanes], along_fwd[1, :, lanes]))
            v = regroup([modes[j * 64 : j * 64 + 64] for j in range(4)])
            for yl in range(2):
                for d in range(2):
                    xbs[c, pl.ds(r + d * 64, 64), pl.ds(yl * 128, 128)] = v[yl * 2 + d]

            @pl.when(k < 4)
            def _():
                pltpu.make_async_remote_copy(
                    src_ref=xbs.at[c, pl.ds(r, 128)],
                    dst_ref=xbr.at[c, pl.ds(pl.multiple_of(mx * 128, 128), 128)],
                    send_sem=xb_send.at[c],
                    recv_sem=xb_recv.at[c],
                    device_id={"row": other * 2 + ml, "col": col},
                    device_id_type=MESH,
                ).start()

            return carry

        lax.fori_loop(1, 5, back, 0)
        mine = pl.ds(pl.multiple_of(mx * 128, 128), 128)
        pltpu.make_async_copy(xbs.at[c, mine], xbr.at[c, mine], xb_recv.at[c]).start()

    def span_back_stage(c):
        wait_all(xbr.at[c], xb_recv.at[c])

        def halve(i, carry):
            rows = pl.ds(pl.multiple_of(i * 128, 128), 128)
            l_hl[0, rows, :], l_hl[1, rows, :] = split(xbr[c, rows, :])
            return carry

        lax.fori_loop(0, 4, halve, 0)

        def one(i, carry):
            rows = pl.ds(pl.multiple_of(i * 128, 128), 128)
            value = dot3((span_fwd[0, rows, :], span_fwd[1, rows, :]), (l_hl[0], l_hl[1]))
            bs[c, 0, rows, :] = value[:, :128]
            bs[c, 1, rows, :] = value[:, 128:]
            return carry

        lax.fori_loop(0, 4, one, 0)
        mine = pl.ds(pl.multiple_of(me * 16, 16), 16)
        pltpu.make_async_copy(
            bs.at[c, ml, pl.ds(pl.multiple_of(col * 16, 16), 16)], br.at[c, mine], b_recv.at[c]
        ).start()

        def send(k, carry):
            other, device = partner(k)
            pltpu.make_async_remote_copy(
                src_ref=bs.at[c, other % 2, pl.ds(pl.multiple_of(other // 2 * 16, 16), 16)],
                dst_ref=br.at[c, mine],
                send_sem=b_send.at[c],
                recv_sem=b_recv.at[c],
                device_id=device,
                device_id_type=MESH,
            ).start()
            return carry

        lax.fori_loop(1, 64, send, 0)

    def collect(c):
        wait_all(br.at[c], b_recv.at[c])
        for g in range(4):
            v = [br[c, pl.ds(4 * g + i, 64, stride=16), :] for i in range(4)]
            for j, u in enumerate(regroup(v)):
                rows = pl.ds(4 * c + j, 64, stride=8)
                t0[g, rows, :] = t0[g, rows, :] + u

    span_stage(0, 0)
    span_stage(1, 0)
    wait_all(vel_v.at[:, :, pl.ds(0, 32)], vel_recv)
    along_stage(0)
    span_back_stage(0)
    span_stage(0, 1)
    span_stage(1, 1)
    collect(0)
    along_stage(1)
    span_back_stage(1)
    collect(1)

    def halve_right(i, carry):
        rows = pl.ds(pl.multiple_of(i * 64, 64), 64)
        for g in range(4):
            lanes = pl.ds(g * 128, 128)
            t_hl[0, rows, lanes], t_hl[1, rows, lanes] = split(t0[g, rows, :])
        return carry

    lax.fori_loop(0, 8, halve_right, 0)

    def basis(i, carry):
        rows = pl.ds(pl.multiple_of(i * 128, 128), 128)
        value = dot3((tb_hl[0, rows, :], tb_hl[1, rows, :]), (t_hl[0], t_hl[1])) * inv_div[rows, :]
        for g in range(4):
            turned = value[:, g * 128 : g * 128 + 128].T
            c_hl[0, pl.ds(g * 128, 128), rows], c_hl[1, pl.ds(g * 128, 128), rows] = split(turned)
        return carry

    lax.fori_loop(0, 4, basis, 0)

    def last(g, carry):
        rows = pl.ds(pl.multiple_of(g * 128, 128), 128)
        value = dot3(
            (c_hl[0, rows, :], c_hl[1, rows, :]), (fb_hl[0], fb_hl[1]), (((1,), (1,)), ((), ()))
        )
        for i in range(4):
            for b in range(4):
                ov[b, pl.ds(4 * g + i, 32, stride=16), :] = value[i * 32 : i * 32 + 32, b * 128 : b * 128 + 128]
        return carry

    lax.fori_loop(0, 4, last, 0)
    results = [pltpu.make_async_copy(ov.at[b], out.at[:, pl.ds(b * 128, 128)], out_sem.at[b]) for b in range(4)]
    for result in results:
        result.start()

    wait_all(vel_v.at[:, :, pl.ds(0, 32)], vel_send)
    for c in range(2):
        for f in range(2):
            wait_all(fs.at[f, c, pl.ds(0, 63)], f_send.at[f, c])
        for h in range(3):
            wait_all(xs.at[c, h, pl.ds(0, 384)], x_send.at[c, h])
        wait_all(xbs.at[c, pl.ds(0, 384)], xb_send.at[c])
        wait_all(br.at[c, pl.ds(0, 1008)], b_send.at[c])
    for result in results:
        result.wait()


def shards(theta_hat, velocity, wall_derivative, to_basis, from_basis, eigenvalues):
    tables = span_tables() + along_tables()
    tables = [jnp.asarray(t) for t in tables]
    vm = pltpu.VMEM
    table = vm((2, 512, 512), BF16)
    square = vm((512, 512), F32)
    blocked = vm((4, 512, 128), F32)
    dma = pltpu.SemaphoreType.DMA
    result = pl.pallas_call(
        kernel,
        out_shape=jax.ShapeDtypeStruct((512, 512), F32),
        in_specs=[pl.BlockSpec(memory_space=pl.ANY)] * 12,
        out_specs=pl.BlockSpec(memory_space=pl.ANY),
        scratch_shapes=[
            blocked, blocked, square, square, square, vm((1, 512), F32), vm((3, 4, 64, 8, 128), F32),
            table, table, table, table, table, table,
            table, table, table, table, square,
            vm((2, 2, 64, 16, 128), F32),
            vm((2, 2, 1024, 128), F32),
            vm((2, 512, 256), BF16),
            vm((2, 3, 512, 256), F32),
            vm((2, 3, 512, 256), F32),
            vm((3, 2, 256, 512), BF16),
            vm((2, 256, 512), BF16),
            vm((2, 512, 256), F32),
            vm((2, 512, 256), F32),
            vm((2, 512, 256), BF16),
            vm((2, 2, 512, 128), F32),
            vm((2, 1024, 128), F32),
            table,
            blocked,
            dma((18,)), dma(()), dma(()), dma((2, 2)), dma((2, 2)), dma((2, 3)), dma((2, 3)),
            dma((2,)), dma((2,)), dma((2,)), dma((2,)), dma((4,)),
        ],
        compiler_params=pltpu.CompilerParams(
            collective_id=0, has_side_effects=True, vmem_limit_bytes=VMEM_LIMIT
        ),
        cost_estimate=pl.CostEstimate(flops=8 * 10**9, bytes_accessed=16 * 2**20, transcendentals=0),
    )(
        theta_hat.reshape(512, 512), velocity, wall_derivative, to_basis, from_basis,
        eigenvalues.reshape(1, 512), *tables,
    )
    return result.reshape(32, 2, 8, 512)


def solution(mesh):
    return jax.shard_map(
        shards,
        mesh=mesh,
        in_specs=(P("row", None, "col", None), P(None, "row", "col", None), P(), P(), P(), P()),
        out_specs=P("row", None, "col", None),
        check_vma=False,
    )
```

profile of v0, /device:TPU:1, one launch (start us, length us, event | category | flops | bytes accessed | tf_op | source)
XLA Modules:
  0.0 140.7 jit_solution(10048913148085695839)
XLA Ops:
  0.0 138.4 %shard_map.118 = f32[512,512]{1,0:T(8,128)} custom-call(f32[512,512]{1,0:T(8,128)} %bitcast.4, f32[3,32,16,512]{3,2,1,0:T(8,128)} %velocity.1, f32[512,512]{1,0:T(8,128)} %wall.1, f32[512,512]{1,0:T(8,128)} %to_basis.1, f32[512,512]{1,0:T(8,128)} %from_basis.1, f32[1,512]{1,0:T(1,128)} %bitcast.5, bf16[2,512,512]{2,1,0:T(8,128)(2,1)} %constant.12.clone.span_inv_h, ...), custom_call_target="tpu_custom_call" | custom-call | flops 8000000000 | bytes 16777216 | tf_op jit(solution)/shard_map/pallas_call | solution.py:482
  138.4 2.3 %copy.14 = f32[32,2,8,512]{3,2,1,0:T(8,128)} copy(f32[32,2,8,512]{3,2,1,0:T(8,128)} %bitcast.3) | data formatting | bytes 2097152
where the time goes:
time: 141 us
  Pallas kernels  138 us (98%)
  local copies, waits for them, and re-layouts  2.31 us (2%)
    pallas_call x1, Pallas kernels, shards(): pl.pallas_call(kernel, out_shape=jax.ShapeDtypeStruct((512, 512), F32), i...  138 us

commit v1 on v0

--- a/solution.py
+++ b/solution.py
@@ -41,8 +41,8 @@
     factor = 1.0 / math.sqrt(NZ)
     inverse = factor * np.cos(angle + 0.5 * math.pi * (c - d))
     derive = factor * signed * np.cos(angle + 0.5 * math.pi * (c + 1 - d))
-    q = np.arange(NZ).reshape(32, 1, 8, 1, 1, 1)
-    d = np.arange(2).reshape(1, 2, 1, 1, 1, 1)
+    q = np.arange(NZ).reshape(1, 32, 8, 1, 1, 1)
+    d = np.arange(2).reshape(2, 1, 1, 1, 1, 1)
     z = np.arange(NZ).reshape(1, 1, 1, 4, 1, 64)
     c = np.arange(2).reshape(1, 1, 1, 1, 2, 1)
     angle = -2.0 * math.pi * ((z * q) % NZ) / NZ
@@ -51,9 +51,9 @@
 
 
 def along_tables():
-    p = np.arange(KX).reshape(4, 2, 1, 32, 1)
-    d = np.arange(2).reshape(1, 1, 2, 1, 1)
-    x = np.arange(NX).reshape(1, 1, 1, 1, NX)
+    p = np.arange(KX).reshape(2, 2, 2, 1, 32, 1).transpose(0, 2, 1, 3, 4, 5)
+    d = np.arange(2).reshape(1, 1, 1, 2, 1, 1)
+    x = np.arange(NX).reshape(1, 1, 1, 1, 1, NX)
     angle = 2.0 * math.pi * ((p * x) % NX) / NX
     factor = math.sqrt(2.0 / NX)
     inverse = (factor * np.cos(angle + 0.5 * math.pi * d)).reshape(512, 512)
@@ -100,7 +100,7 @@
     th_v, t0, mat_v, tb_v, fb_v, eig_v, vel_v,
     span_inv, span_der, span_fwd, along_inv, along_der, along_fwd,
     d_hl, t_hl, tb_hl, fb_hl, inv_div,
-    fs, fr, x_hl, xs, xr, y_hl, adv_hl, xbs, xbr, l_hl, bs, br, c_hl, ov,
+    fs, fr, x_hl, xs, xr, y_hl, adv_hl, xbs, xbr, bs, br, c_hl, ov,
     load_sem, vel_send, vel_recv, f_send, f_recv, x_send, x_recv, xb_send, xb_recv, b_send, b_recv, out_sem,
 ):
     row = lax.axis_index("row")
@@ -178,7 +178,7 @@
 
     pl.semaphore_wait(barrier, 66)
 
-    def send_fwd(f, c, velocity_too):
+    def send_fwd(f, c, velocity_part):
         mine = pl.ds(pl.multiple_of(me * 16, 16), 16)
         pltpu.make_async_copy(fs.at[f, c, me], fr.at[f, c, mine], f_recv.at[f, c]).start()
 
@@ -195,31 +195,28 @@
             return carry
 
         def piece(i, carry):
-            lax.fori_loop(1 + 4 * i, jnp.minimum(5 + 4 * i, 64), one, 0)
-            send_vel(i)
-            return carry
-
-        if velocity_too:
-            lax.fori_loop(0, 16, piece, 0)
+            lax.fori_loop(1 + 16 * i, jnp.minimum(17 + 16 * i, 64), one, 0)
+            send_vel(i, velocity_part)
+            return carry
+
+        if velocity_part is None:
+            lax.fori_loop(1, 64, one, 0)
         else:
-            lax.fori_loop(1, 64, one, 0)
-
-    def send_vel(i):
+            lax.fori_loop(0, 4, piece, 0)
+
+    def send_vel(i, c):
         pltpu.make_async_remote_copy(
             src_ref=velocity.at[
-                :,
-                pl.ds(i % 4 * 8, 8),
-                pl.ds(pl.multiple_of((1 - ml) * 8, 8), 8),
-                pl.ds(pl.multiple_of(i // 4 * 128, 128), 128),
+                :, :, pl.ds((1 - ml) * 8 + c * 2, 2), pl.ds(pl.multiple_of(i * 128, 128), 128)
             ],
-            dst_ref=vel_v.at[:, i // 4, pl.ds(ml * 32 + i % 4 * 8, 8)],
-            send_sem=vel_send,
-            recv_sem=vel_recv,
+            dst_ref=vel_v.at[:, i, pl.ds(ml * 32, 32), pl.ds(c * 2, 2)],
+            send_sem=vel_send.at[c],
+            recv_sem=vel_recv.at[c],
             device_id={"row": mx * 2 + 1 - ml, "col": col},
             device_id_type=MESH,
         ).start()
 
-    send_fwd(0, 0, False)
+    send_fwd(0, 0, None)
 
     loads[0].wait()
 
@@ -230,9 +227,11 @@
         return carry
 
     lax.fori_loop(0, 4, slope, 0)
-    send_fwd(1, 0, False)
-    send_fwd(0, 1, True)
-    send_fwd(1, 1, False)
+    send_fwd(1, 0, 0)
+    send_fwd(0, 1, 1)
+    send_fwd(1, 1, 2)
+    for i in range(4):
+        send_vel(i, 3)
 
     for copy in loads[1:]:
         copy.wait()
@@ -262,65 +261,62 @@
 
     def span_stage(f, c):
         wait_all(fr.at[f, c], f_recv.at[f, c])
-        for yl in range(2):
-            for qh in range(2):
-                for g in range(2):
-                    v = [
-                        fr[f, c, pl.ds(yl * 16 + g * 8 + qh * 4 + j, 32, stride=32), :] for j in range(4)
-                    ]
-                    for i, u in enumerate(regroup(v)):
-                        r = (qh * 8 + g * 4 + i) * 32
-                        x_hl[0, pl.ds(r, 32), pl.ds(yl * 128, 128)], x_hl[1, pl.ds(r, 32), pl.ds(yl * 128, 128)] = split(u)
-
-        def lift(table, h):
-            def one(k, carry):
-                other = wrap(mx + k, 4)
-                r = pl.multiple_of(other * 128, 128)
-                xs[c, h, pl.ds(r, 128), :] = dot3(
-                    (table[0, pl.ds(r, 128), :], table[1, pl.ds(r, 128), :]), (x_hl[0], x_hl[1])
-                )
-                pltpu.make_async_remote_copy(
-                    src_ref=xs.at[c, h, pl.ds(r, 128)],
-                    dst_ref=xr.at[c, h, pl.ds(pl.multiple_of(mx * 128, 128), 128)],
-                    send_sem=x_send.at[c, h],
-                    recv_sem=x_recv.at[c, h],
-                    device_id={"row": other * 2 + ml, "col": col},
-                    device_id_type=MESH,
-                ).start()
+
+        def sub(i, carry):
+            part = 2 * c + i
+
+            def collect_modes(t, carry):
+                start = (t % 2) * 8 + (t // 2) * 4 + 2 * i
+                v = [fr[f, c, pl.ds(start + 16 * yl + j, 32, stride=32), :] for yl in range(2) for j in range(2)]
+                for n, u in enumerate(regroup(v)):
+                    rows = pl.ds(pl.multiple_of(t * 128 + n * 32, 32), 32)
+                    x_hl[0, rows, :], x_hl[1, rows, :] = split(u)
                 return carry
 
-            lax.fori_loop(1, 4, one, 0)
-            r = pl.multiple_of(mx * 128, 128)
-            xs[c, h, pl.ds(r, 128), :] = dot3(
-                (table[0, pl.ds(r, 128), :], table[1, pl.ds(r, 128), :]), (x_hl[0], x_hl[1])
-            )
-            pltpu.make_async_copy(xs.at[c, h, pl.ds(r, 128)], xr.at[c, h, pl.ds(r, 128)], x_recv.at[c, h]).start()
-
-        if f == 0:
-            lift(span_inv, 0)
-            lift(span_der, 1)
-        else:
-            lift(span_inv, 2)
-
-    def gather_lines(c, h):
-        wait_all(xr.at[c, h], x_recv.at[c, h])
-
-        def one(x, carry):
-            r = pl.multiple_of(x * 128, 128)
-            v = [xr[c, h, pl.ds(r + d * 64, 64), pl.ds(yl * 128, 128)] for yl in range(2) for d in range(2)]
-            for j, u in enumerate(regroup(v)):
-                lanes = pl.ds(r, 128)
-                y_hl[h, 0, pl.ds(j * 64, 64), lanes], y_hl[h, 1, pl.ds(j * 64, 64), lanes] = split(u)
-            return carry
-
-        lax.fori_loop(0, 4, one, 0)
-
-    def along_stage(c):
+            lax.fori_loop(0, 4, collect_modes, 0)
+            for table, h in ((span_inv, 0), (span_der, 1)) if f == 0 else ((span_inv, 2),):
+                xs[part, h] = dot3((table[0], table[1]), (x_hl[0], x_hl[1]))
+                mine = pl.ds(pl.multiple_of(mx * 128, 128), 128)
+
+                def send(k, carry):
+                    other = wrap(mx + k, 4)
+                    pltpu.make_async_remote_copy(
+                        src_ref=xs.at[part, h, pl.ds(pl.multiple_of(other * 128, 128), 128)],
+                        dst_ref=xr.at[part, h, mine],
+                        send_sem=x_send.at[part, h],
+                        recv_sem=x_recv.at[part, h],
+                        device_id={"row": other * 2 + ml, "col": col},
+                        device_id_type=MESH,
+                    ).start()
+                    return carry
+
+                lax.fori_loop(1, 4, send, 0)
+                pltpu.make_async_copy(xs.at[part, h, mine], xr.at[part, h, mine], x_recv.at[part, h]).start()
+            return carry
+
+        lax.fori_loop(0, 2, sub, 0)
+
+    def along_stage(part):
         flat = vel_v.reshape(3, 4, 512, 128)
+
+        def gather_lines(n, carry):
+            for h in range(3):
+                v = [
+                    xr[part, h, pl.ds(pl.multiple_of(n * 256 + i * 64, 64), 64), :] for i in range(4)
+                ]
+                for i, u in enumerate(regroup(v)):
+                    yl, j = i // 2, i % 2
+                    rows = pl.ds(j * 64, 64)
+                    lanes = pl.ds(pl.multiple_of(n * 256 + yl * 128, 128), 128)
+                    y_hl[h, 0, rows, lanes], y_hl[h, 1, rows, lanes] = split(u)
+            return carry
+
         for h in range(3):
-            gather_lines(c, h)
-
-        def one(n, carry):
+            wait_all(xr.at[part, h], x_recv.at[part, h])
+        lax.fori_loop(0, 2, gather_lines, 0)
+        wait_all(vel_v.at[:, :, pl.ds(0, 32), pl.ds(0, 2)], vel_recv.at[part])
+
+        def product(n, carry):
             lanes = pl.ds(pl.multiple_of(n * 256, 256), 256)
             total = None
             for h, (table, component) in enumerate(((along_der, 0), (along_inv, 2), (along_inv, 1))):
@@ -328,7 +324,7 @@
                 speed = jnp.concatenate(
                     [
                         jnp.concatenate(
-                            [flat[component, 2 * n + b, pl.ds(4 * c + j, 64, stride=8), :] for j in range(4)], axis=0
+                            [flat[component, 2 * n + b, pl.ds(2 * part + j, 64, stride=8), :] for j in range(2)], axis=0
                         )
                         for b in range(2)
                     ],
@@ -339,65 +335,53 @@
             adv_hl[0, :, lanes], adv_hl[1, :, lanes] = split(total)
             return carry
 
-        lax.fori_loop(0, 2, one, 0)
-
-        def back(k, carry):
+        lax.fori_loop(0, 2, product, 0)
+
+        def back(n, carry):
+            lanes = pl.ds(pl.multiple_of(n * 256, 256), 256)
+            modes = dot3((adv_hl[0], adv_hl[1]), (along_fwd[0, :, lanes], along_fwd[1, :, lanes]))
+            v = [modes[j * 64 : j * 64 + 64, yl * 128 : yl * 128 + 128] for yl in range(2) for j in range(2)]
+            for i, u in enumerate(regroup(v)):
+                xbs[part, pl.ds(pl.multiple_of(n * 256 + i * 64, 64), 64), :] = u
+            return carry
+
+        lax.fori_loop(0, 2, back, 0)
+        mine = pl.ds(pl.multiple_of(mx * 128, 128), 128)
+
+        def send(k, carry):
             other = wrap(mx + k, 4)
-            r = pl.multiple_of(other * 128, 128)
-            lanes = pl.ds(r, 128)
-            modes = dot3((adv_hl[0], adv_hl[1]), (along_fwd[0, :, lanes], along_fwd[1, :, lanes]))
-            v = regroup([modes[j * 64 : j * 64 + 64] for j in range(4)])
-            for yl in range(2):
-                for d in range(2):
-                    xbs[c, pl.ds(r + d * 64, 64), pl.ds(yl * 128, 128)] = v[yl * 2 + d]
-
-            @pl.when(k < 4)
-            def _():
-                pltpu.make_async_remote_copy(
-                    src_ref=xbs.at[c, pl.ds(r, 128)],
-                    dst_ref=xbr.at[c, pl.ds(pl.multiple_of(mx * 128, 128), 128)],
-                    send_sem=xb_send.at[c],
-                    recv_sem=xb_recv.at[c],
-                    device_id={"row": other * 2 + ml, "col": col},
-                    device_id_type=MESH,
-                ).start()
-
-            return carry
-
-        lax.fori_loop(1, 5, back, 0)
-        mine = pl.ds(pl.multiple_of(mx * 128, 128), 128)
-        pltpu.make_async_copy(xbs.at[c, mine], xbr.at[c, mine], xb_recv.at[c]).start()
-
-    def span_back_stage(c):
-        wait_all(xbr.at[c], xb_recv.at[c])
-
-        def halve(i, carry):
-            rows = pl.ds(pl.multiple_of(i * 128, 128), 128)
-            l_hl[0, rows, :], l_hl[1, rows, :] = split(xbr[c, rows, :])
-            return carry
-
-        lax.fori_loop(0, 4, halve, 0)
-
-        def one(i, carry):
-            rows = pl.ds(pl.multiple_of(i * 128, 128), 128)
-            value = dot3((span_fwd[0, rows, :], span_fwd[1, rows, :]), (l_hl[0], l_hl[1]))
-            bs[c, 0, rows, :] = value[:, :128]
-            bs[c, 1, rows, :] = value[:, 128:]
-            return carry
-
-        lax.fori_loop(0, 4, one, 0)
-        mine = pl.ds(pl.multiple_of(me * 16, 16), 16)
+            pltpu.make_async_remote_copy(
+                src_ref=xbs.at[part, pl.ds(pl.multiple_of(other * 128, 128), 128)],
+                dst_ref=xbr.at[part, mine],
+                send_sem=xb_send.at[part],
+                recv_sem=xb_recv.at[part],
+                device_id={"row": other * 2 + ml, "col": col},
+                device_id_type=MESH,
+            ).start()
+            return carry
+
+        lax.fori_loop(1, 4, send, 0)
+        pltpu.make_async_copy(xbs.at[part, mine], xbr.at[part, mine], xb_recv.at[part]).start()
+
+    def span_back_stage(part):
+        wait_all(xbr.at[part], xb_recv.at[part])
+        value = dot3((span_fwd[0], span_fwd[1]), split(xbr[part]))
+        real, imag = value[:256], value[256:]
+        low = lax.broadcasted_iota(jnp.int32, (256, 128), 1) < 64
+        bs[part, 0] = jnp.where(low, real, pltpu.roll(imag, 64, 1))
+        bs[part, 1] = jnp.where(low, pltpu.roll(real, 64, 1), imag)
+        mine = pl.ds(pl.multiple_of(me * 8, 8), 8)
         pltpu.make_async_copy(
-            bs.at[c, ml, pl.ds(pl.multiple_of(col * 16, 16), 16)], br.at[c, mine], b_recv.at[c]
+            bs.at[part, ml, pl.ds(pl.multiple_of(col * 8, 8), 8)], br.at[part, mine], b_recv.at[part]
         ).start()
 
         def send(k, carry):
             other, device = partner(k)
             pltpu.make_async_remote_copy(
-                src_ref=bs.at[c, other % 2, pl.ds(pl.multiple_of(other // 2 * 16, 16), 16)],
-                dst_ref=br.at[c, mine],
-                send_sem=b_send.at[c],
-                recv_sem=b_recv.at[c],
+                src_ref=bs.at[part, other % 2, pl.ds(pl.multiple_of(other // 2 * 8, 8), 8)],
+                dst_ref=br.at[part, mine],
+                send_sem=b_send.at[part],
+                recv_sem=b_recv.at[part],
                 device_id=device,
                 device_id_type=MESH,
             ).start()
@@ -405,25 +389,31 @@
 
         lax.fori_loop(1, 64, send, 0)
 
-    def collect(c):
-        wait_all(br.at[c], b_recv.at[c])
-        for g in range(4):
-            v = [br[c, pl.ds(4 * g + i, 64, stride=16), :] for i in range(4)]
-            for j, u in enumerate(regroup(v)):
-                rows = pl.ds(4 * c + j, 64, stride=8)
+    def collect(part):
+        wait_all(br.at[part], b_recv.at[part])
+        for n in range(2):
+            v = [br[part, pl.ds(4 * n + i, 64, stride=8), :] for i in range(4)]
+            for i, u in enumerate(regroup(v)):
+                rows = pl.ds(2 * part + i % 2, 64, stride=8)
+                g = i // 2 * 2 + n
                 t0[g, rows, :] = t0[g, rows, :] + u
 
     span_stage(0, 0)
     span_stage(1, 0)
-    wait_all(vel_v.at[:, :, pl.ds(0, 32)], vel_recv)
     along_stage(0)
+    along_stage(1)
     span_back_stage(0)
     span_stage(0, 1)
+    span_back_stage(1)
     span_stage(1, 1)
+    along_stage(2)
     collect(0)
-    along_stage(1)
-    span_back_stage(1)
+    along_stage(3)
+    span_back_stage(2)
     collect(1)
+    span_back_stage(3)
+    collect(2)
+    collect(3)
 
     def halve_right(i, carry):
         rows = pl.ds(pl.multiple_of(i * 64, 64), 64)
@@ -459,14 +449,15 @@
     for result in results:
         result.start()
 
-    wait_all(vel_v.at[:, :, pl.ds(0, 32)], vel_send)
     for c in range(2):
         for f in range(2):
             wait_all(fs.at[f, c, pl.ds(0, 63)], f_send.at[f, c])
+    for part in range(4):
+        wait_all(vel_v.at[:, :, pl.ds(0, 32), pl.ds(0, 2)], vel_send.at[part])
         for h in range(3):
-            wait_all(xs.at[c, h, pl.ds(0, 384)], x_send.at[c, h])
-        wait_all(xbs.at[c, pl.ds(0, 384)], xb_send.at[c])
-        wait_all(br.at[c, pl.ds(0, 1008)], b_send.at[c])
+            wait_all(xs.at[part, h, pl.ds(0, 384)], x_send.at[part, h])
+        wait_all(xbs.at[part, pl.ds(0, 384)], xb_send.at[part])
+        wait_all(br.at[part, pl.ds(0, 504)], b_send.at[part])
     for result in results:
         result.wait()
 
@@ -490,20 +481,19 @@
             table, table, table, table, square,
             vm((2, 2, 64, 16, 128), F32),
             vm((2, 2, 1024, 128), F32),
-            vm((2, 512, 256), BF16),
-            vm((2, 3, 512, 256), F32),
-            vm((2, 3, 512, 256), F32),
-            vm((3, 2, 256, 512), BF16),
-            vm((2, 256, 512), BF16),
-            vm((2, 512, 256), F32),
-            vm((2, 512, 256), F32),
-            vm((2, 512, 256), BF16),
-            vm((2, 2, 512, 128), F32),
-            vm((2, 1024, 128), F32),
+            vm((2, 512, 128), BF16),
+            vm((4, 3, 512, 128), F32),
+            vm((4, 3, 512, 128), F32),
+            vm((3, 2, 128, 512), BF16),
+            vm((2, 128, 512), BF16),
+            vm((4, 512, 128), F32),
+            vm((4, 512, 128), F32),
+            vm((4, 2, 256, 128), F32),
+            vm((4, 512, 128), F32),
             table,
             blocked,
-            dma((18,)), dma(()), dma(()), dma((2, 2)), dma((2, 2)), dma((2, 3)), dma((2, 3)),
-            dma((2,)), dma((2,)), dma((2,)), dma((2,)), dma((4,)),
+            dma((18,)), dma((4,)), dma((4,)), dma((2, 2)), dma((2, 2)), dma((4, 3)), dma((4, 3)),
+            dma((4,)), dma((4,)), dma((4,)), dma((4,)), dma((4,)),
         ],
         compiler_params=pltpu.CompilerParams(
             collective_id=0, has_side_effects=True, vmem_limit_bytes=VMEM_LIMIT

time: 141 us -> 107 us (0.76)
  Pallas kernels: 138 us -> 104 us
    pallas_call x1, Pallas kernels: 138 us -> 104 us  [shards(): pl.pallas_call(kernel, out_shape=jax.ShapeDtypeStruct((512, 512), F32), i...]
where the time goes in v1:
time: 107 us
  Pallas kernels  104 us (97%)
  local copies, waits for them, and re-layouts  2.31 us (2%)
    pallas_call x1, Pallas kernels, shards(): pl.pallas_call(kernel, out_shape=jax.ShapeDtypeStruct((512, 512), F32), i...  104 us
    unnamed x1, local copies, waits for them, and re-layouts  2.31 us

profile of v1, /device:TPU:1, one launch (start us, length us, event | category | flops | bytes accessed | tf_op | source)
XLA Modules:
  0.0 106.8 jit_solution(16412090938469267100)
XLA Ops:
  0.0 104.5 %shard_map.118 = f32[512,512]{1,0:T(8,128)} custom-call(f32[512,512]{1,0:T(8,128)} %bitcast.4, f32[3,32,16,512]{3,2,1,0:T(8,128)} %velocity.1, f32[512,512]{1,0:T(8,128)} %wall.1, f32[512,512]{1,0:T(8,128)} %to_basis.1, f32[512,512]{1,0:T(8,128)} %from_basis.1, f32[1,512]{1,0:T(1,128)} %bitcast.5, bf16[2,512,512]{2,1,0:T(8,128)(2,1)} %constant.12.clone.span_inv_h, ...), custom_call_target="tpu_custom_call" | custom-call | flops 8000000000 | bytes 16777216 | tf_op jit(solution)/shard_map/pallas_call | solution.py:473
  104.5 2.3 %copy.14 = f32[32,2,8,512]{3,2,1,0:T(8,128)} copy(f32[32,2,8,512]{3,2,1,0:T(8,128)} %bitcast.3) | data formatting | bytes 2097152

commit v2 on v1

--- a/solution.py
+++ b/solution.py
@@ -89,6 +89,9 @@
     )
 
 
+LAST = (((1,), (1,)), ((), ()))
+
+
 def wrap(value, n):
     return jnp.where(value >= n, value - n, value)
 
@@ -100,13 +103,13 @@
     th_v, t0, mat_v, tb_v, fb_v, eig_v, vel_v,
     span_inv, span_der, span_fwd, along_inv, along_der, along_fwd,
     d_hl, t_hl, tb_hl, fb_hl, inv_div,
-    fs, fr, x_hl, xs, xr, y_hl, adv_hl, xbs, xbr, bs, br, c_hl, ov,
+    fs, fr, x_hl, xs, xr, y_hl, grad, adv_hl, xbs, xbr, bs, br, c_hl, r_v, perm, tbp_hl, acc, ov,
     load_sem, vel_send, vel_recv, f_send, f_recv, x_send, x_recv, xb_send, xb_recv, b_send, b_recv, out_sem,
 ):
     row = lax.axis_index("row")
     col = lax.axis_index("col")
-    mx = row // 2
-    ml = row % 2
+    mx = lax.div(row, 2)
+    ml = lax.rem(row, 2)
     me = col * 2 + ml
 
     loads = [
@@ -137,7 +140,7 @@
 
     def partner(k):
         other = wrap(me + k, 64)
-        return other, {"row": mx * 2 + other % 2, "col": other // 2}
+        return other, {"row": mx * 2 + lax.rem(other, 2), "col": lax.div(other, 2)}
 
     def greet(k, carry):
         pl.semaphore_signal(barrier, inc=1, device_id=partner(k)[1], device_id_type=MESH)
@@ -200,7 +203,7 @@
             return carry
 
         if velocity_part is None:
-            lax.fori_loop(1, 64, one, 0)
+            lax.fori_loop(1, 64, one, 0, unroll=7)
         else:
             lax.fori_loop(0, 4, piece, 0)
 
@@ -229,32 +232,39 @@
     lax.fori_loop(0, 4, slope, 0)
     send_fwd(1, 0, 0)
     send_fwd(0, 1, 1)
-    send_fwd(1, 1, 2)
-    for i in range(4):
-        send_vel(i, 3)
-
-    for copy in loads[1:]:
-        copy.wait()
-
-    def halves(i, carry):
-        r = pl.multiple_of(i * 64, 64)
-        tb_hl[0, pl.ds(r, 64), :], tb_hl[1, pl.ds(r, 64), :] = split(tb_v[pl.ds(r, 64), :])
-        fb_hl[0, pl.ds(r, 64), :], fb_hl[1, pl.ds(r, 64), :] = split(fb_v[pl.ds(r, 64), :])
-        return carry
-
-    lax.fori_loop(0, 8, halves, 0)
-    lane = lax.broadcasted_iota(jnp.int32, (1, 512), 1)
-    along_wave = WAVE_ALONG * (row * 32 + lane % 32).astype(F32)
-    span_id = col * 8 + (lane // 32) % 8
-    span_wave = WAVE_SPAN * jnp.where(span_id < NZ // 2, span_id, span_id - NZ).astype(F32)
-    waves = along_wave * along_wave + span_wave * span_wave
-    for kb in range(4):
-        column = jnp.broadcast_to(eig_v[:, pl.ds(kb * 128, 128)], (128, 128)).T
-        for g in range(4):
-            total = waves[:, g * 128 : g * 128 + 128] + column
-            inv_div[pl.ds(kb * 128, 128), pl.ds(g * 128, 128)] = 1.0 / (1.0 + TIME_STEP * DIFFUSIVITY * total)
-    for copy in own_vel:
-        copy.wait()
+
+    def prepare_basis():
+        def halves(i, carry):
+            rows = pl.ds(pl.multiple_of(i * 64, 64), 64)
+            tb_hl[0, rows, :], tb_hl[1, rows, :] = split(tb_v[rows, :])
+            fb_hl[0, rows, :], fb_hl[1, rows, :] = split(fb_v[rows, :])
+            j = lax.broadcasted_iota(jnp.int32, (64, 512), 0) + i * 64
+            n = lax.broadcasted_iota(jnp.int32, (64, 512), 1)
+            perm[rows, :] = jnp.where(j == n % 64 * 8 + n // 64, 1.0, 0.0).astype(BF16)
+            return carry
+
+        lax.fori_loop(0, 8, halves, 0)
+        for i in range(2):
+            tbp_hl[i] = jnp.dot(tb_hl[i], perm[...], preferred_element_type=F32).astype(BF16)
+
+    def prepare_divisor():
+        def divisor(i, carry):
+            rows = pl.ds(pl.multiple_of(i * 128, 128), 128)
+            r = lax.broadcasted_iota(jnp.int32, (128, 512), 0) + i * 128
+            along_wave = WAVE_ALONG * (row * 32 + r // 16).astype(F32)
+            span_id = col * 8 + r % 8
+            span_wave = WAVE_SPAN * jnp.where(span_id < NZ // 2, span_id, span_id - NZ).astype(F32)
+            total = along_wave * along_wave + span_wave * span_wave + eig_v[...]
+            inv_div[rows, :] = 1.0 / (1.0 + TIME_STEP * DIFFUSIVITY * total)
+            for b in range(4):
+                lanes = pl.ds(b * 128, 128)
+                c_hl[0, rows, lanes], c_hl[1, rows, lanes] = split(th_v[b, rows, :])
+            return carry
+
+        lax.fori_loop(0, 4, divisor, 0)
+
+    def prepare_theta():
+        acc[...] = dot3((c_hl[0], c_hl[1]), (tb_hl[0], tb_hl[1]), LAST)
 
     def wait_all(ref, sem):
         pltpu.make_async_copy(ref, ref, sem).wait()
@@ -296,9 +306,7 @@
 
         lax.fori_loop(0, 2, sub, 0)
 
-    def along_stage(part):
-        flat = vel_v.reshape(3, 4, 512, 128)
-
+    def gradient_stage(part):
         def gather_lines(n, carry):
             for h in range(3):
                 v = [
@@ -314,28 +322,27 @@
         for h in range(3):
             wait_all(xr.at[part, h], x_recv.at[part, h])
         lax.fori_loop(0, 2, gather_lines, 0)
+        for h, table in enumerate((along_der, along_inv, along_inv)):
+            grad[part % 2, h] = dot3((y_hl[h, 0], y_hl[h, 1]), (table[0], table[1]))
+
+    def along_stage(part):
+        flat = vel_v.reshape(3, 4, 512, 128)
         wait_all(vel_v.at[:, :, pl.ds(0, 32), pl.ds(0, 2)], vel_recv.at[part])
 
-        def product(n, carry):
-            lanes = pl.ds(pl.multiple_of(n * 256, 256), 256)
-            total = None
-            for h, (table, component) in enumerate(((along_der, 0), (along_inv, 2), (along_inv, 1))):
-                grad = dot3((y_hl[h, 0], y_hl[h, 1]), (table[0, :, lanes], table[1, :, lanes]))
-                speed = jnp.concatenate(
-                    [
-                        jnp.concatenate(
-                            [flat[component, 2 * n + b, pl.ds(2 * part + j, 64, stride=8), :] for j in range(2)], axis=0
-                        )
-                        for b in range(2)
-                    ],
-                    axis=1,
+        def product(b, carry):
+            lanes = pl.ds(pl.multiple_of(b * 128, 128), 128)
+            for j in range(2):
+                rows = pl.ds(j * 64, 64)
+                points = pl.ds(2 * part + j, 64, stride=8)
+                total = (
+                    grad[part % 2, 0, rows, lanes] * flat[0, b, points, :]
+                    + grad[part % 2, 2, rows, lanes] * flat[1, b, points, :]
+                    + grad[part % 2, 1, rows, lanes] * flat[2, b, points, :]
                 )
-                term = grad * speed
-                total = term if total is None else total + term
-            adv_hl[0, :, lanes], adv_hl[1, :, lanes] = split(total)
-            return carry
-
-        lax.fori_loop(0, 2, product, 0)
+                adv_hl[0, rows, lanes], adv_hl[1, rows, lanes] = split(total)
+            return carry
+
+        lax.fori_loop(0, 4, product, 0)
 
         def back(n, carry):
             lanes = pl.ds(pl.multiple_of(n * 256, 256), 256)
@@ -378,7 +385,7 @@
         def send(k, carry):
             other, device = partner(k)
             pltpu.make_async_remote_copy(
-                src_ref=bs.at[part, other % 2, pl.ds(pl.multiple_of(other // 2 * 8, 8), 8)],
+                src_ref=bs.at[part, lax.rem(other, 2), pl.ds(pl.multiple_of(lax.div(other, 2) * 8, 8), 8)],
                 dst_ref=br.at[part, mine],
                 send_sem=b_send.at[part],
                 recv_sem=b_recv.at[part],
@@ -387,67 +394,56 @@
             ).start()
             return carry
 
-        lax.fori_loop(1, 64, send, 0)
+        lax.fori_loop(1, 64, send, 0, unroll=7)
 
     def collect(part):
         wait_all(br.at[part], b_recv.at[part])
         for n in range(2):
             v = [br[part, pl.ds(4 * n + i, 64, stride=8), :] for i in range(4)]
-            for i, u in enumerate(regroup(v)):
-                rows = pl.ds(2 * part + i % 2, 64, stride=8)
-                g = i // 2 * 2 + n
-                t0[g, rows, :] = t0[g, rows, :] + u
-
+            u = regroup(v)
+            for c in range(2):
+                turned = jnp.concatenate([u[2 * c], u[2 * c + 1]], axis=0).T
+                for i in range(4):
+                    r_v[pl.ds(8 * c + 4 * n + i, 32, stride=16), :] = turned[i * 32 : i * 32 + 32]
+        lanes = pl.ds(part * 128, 128)
+        return acc[...] + dot3(split(r_v[...]), (tbp_hl[0, :, lanes], tbp_hl[1, :, lanes]), LAST)
+
+    for copy in loads[1:6]:
+        copy.wait()
     span_stage(0, 0)
+    send_fwd(1, 1, 2)
+    for i in range(4):
+        send_vel(i, 3)
+    for copy in loads[6:] + own_vel:
+        copy.wait()
+    prepare_basis()
     span_stage(1, 0)
+    prepare_divisor()
+    gradient_stage(0)
     along_stage(0)
+    gradient_stage(1)
     along_stage(1)
+    prepare_theta()
+    span_stage(0, 1)
     span_back_stage(0)
-    span_stage(0, 1)
     span_back_stage(1)
     span_stage(1, 1)
+    gradient_stage(2)
     along_stage(2)
-    collect(0)
+    gradient_stage(3)
     along_stage(3)
     span_back_stage(2)
-    collect(1)
     span_back_stage(3)
-    collect(2)
-    collect(3)
-
-    def halve_right(i, carry):
-        rows = pl.ds(pl.multiple_of(i * 64, 64), 64)
-        for g in range(4):
-            lanes = pl.ds(g * 128, 128)
-            t_hl[0, rows, lanes], t_hl[1, rows, lanes] = split(t0[g, rows, :])
-        return carry
-
-    lax.fori_loop(0, 8, halve_right, 0)
-
-    def basis(i, carry):
-        rows = pl.ds(pl.multiple_of(i * 128, 128), 128)
-        value = dot3((tb_hl[0, rows, :], tb_hl[1, rows, :]), (t_hl[0], t_hl[1])) * inv_div[rows, :]
-        for g in range(4):
-            turned = value[:, g * 128 : g * 128 + 128].T
-            c_hl[0, pl.ds(g * 128, 128), rows], c_hl[1, pl.ds(g * 128, 128), rows] = split(turned)
-        return carry
-
-    lax.fori_loop(0, 4, basis, 0)
-
-    def last(g, carry):
-        rows = pl.ds(pl.multiple_of(g * 128, 128), 128)
-        value = dot3(
-            (c_hl[0, rows, :], c_hl[1, rows, :]), (fb_hl[0], fb_hl[1]), (((1,), (1,)), ((), ()))
-        )
-        for i in range(4):
-            for b in range(4):
-                ov[b, pl.ds(4 * g + i, 32, stride=16), :] = value[i * 32 : i * 32 + 32, b * 128 : b * 128 + 128]
-        return carry
-
-    lax.fori_loop(0, 4, last, 0)
-    results = [pltpu.make_async_copy(ov.at[b], out.at[:, pl.ds(b * 128, 128)], out_sem.at[b]) for b in range(4)]
-    for result in results:
-        result.start()
+    acc[...] = collect(0)
+    acc[...] = collect(1)
+    acc[...] = collect(2)
+    c_hl[0], c_hl[1] = split(collect(3) * inv_div[...])
+    results = []
+    for half in range(2):
+        points = pl.ds(half * 256, 256)
+        ov[:, points] = dot3((c_hl[0], c_hl[1]), (fb_hl[0, points, :], fb_hl[1, points, :]), LAST)
+        results.append(pltpu.make_async_copy(ov.at[:, points], out.at[:, points], out_sem.at[half]))
+        results[-1].start()
 
     for c in range(2):
         for f in range(2):
@@ -485,13 +481,18 @@
             vm((4, 3, 512, 128), F32),
             vm((4, 3, 512, 128), F32),
             vm((3, 2, 128, 512), BF16),
+            vm((2, 3, 128, 512), F32),
             vm((2, 128, 512), BF16),
             vm((4, 512, 128), F32),
             vm((4, 512, 128), F32),
             vm((4, 2, 256, 128), F32),
             vm((4, 512, 128), F32),
             table,
-            blocked,
+            vm((512, 128), F32),
+            vm((512, 512), BF16),
+            table,
+            square,
+            square,
             dma((18,)), dma((4,)), dma((4,)), dma((2, 2)), dma((2, 2)), dma((4, 3)), dma((4, 3)),
             dma((4,)), dma((4,)), dma((4,)), dma((4,)), dma((4,)),
         ],

time: 107 us -> 101 us (0.944)
  Pallas kernels: 104 us -> 98.5 us
    pallas_call x1, Pallas kernels: 104 us -> 98.5 us  [shards(): pl.pallas_call(kernel, out_shape=jax.ShapeDtypeStruct((512, 512), F32), i...]
where the time goes in v2:
time: 101 us
  Pallas kernels  98.5 us (98%)
  local copies, waits for them, and re-layouts  2.31 us (2%)
    pallas_call x1, Pallas kernels, shards(): pl.pallas_call(kernel, out_shape=jax.ShapeDtypeStruct((512, 512), F32), i...  98.5 us
    unnamed x1, local copies, waits for them, and re-layouts  2.31 us

profile of v2, /device:TPU:1, one launch (start us, length us, event | category | flops | bytes accessed | tf_op | source)
XLA Modules:
  0.0 100.8 jit_solution(3753611971236835238)
XLA Ops:
  0.0 98.5 %shard_map.118 = f32[512,512]{1,0:T(8,128)} custom-call(f32[512,512]{1,0:T(8,128)} %bitcast.4, f32[3,32,16,512]{3,2,1,0:T(8,128)} %velocity.1, f32[512,512]{1,0:T(8,128)} %wall.1, f32[512,512]{1,0:T(8,128)} %to_basis.1, f32[512,512]{1,0:T(8,128)} %from_basis.1, f32[1,512]{1,0:T(1,128)} %bitcast.5, bf16[2,512,512]{2,1,0:T(8,128)(2,1)} %constant.12.clone.span_inv_h, ...), custom_call_target="tpu_custom_call" | custom-call | flops 8000000000 | bytes 16777216 | tf_op jit(solution)/shard_map/pallas_call | solution.py:469
  98.5 2.3 %copy.14 = f32[32,2,8,512]{3,2,1,0:T(8,128)} copy(f32[32,2,8,512]{3,2,1,0:T(8,128)} %bitcast.3) | data formatting | bytes 2097152

commit v3 on v2

--- a/solution.py
+++ b/solution.py
@@ -123,7 +123,9 @@
         )
     ]
     first = [
-        pltpu.make_async_copy(theta.at[:, pl.ds(b * 128, 128)], th_v.at[b], load_sem.at[10 + b]) for b in range(4)
+        pltpu.make_async_copy(
+            theta.at[:, pl.ds(b * 128, 128)], th_v.at[b, pl.ds(0, 512)], load_sem.at[10 + b]
+        ) for b in range(4)
     ]
     own_vel = [
         pltpu.make_async_copy(
@@ -270,7 +272,7 @@
         pltpu.make_async_copy(ref, ref, sem).wait()
 
     def span_stage(f, c):
-        wait_all(fr.at[f, c], f_recv.at[f, c])
+        wait_all(fr.at[f, c, pl.ds(0, 1024)], f_recv.at[f, c])
 
         def sub(i, carry):
             part = 2 * c + i
@@ -326,7 +328,7 @@
             grad[part % 2, h] = dot3((y_hl[h, 0], y_hl[h, 1]), (table[0], table[1]))
 
     def along_stage(part):
-        flat = vel_v.reshape(3, 4, 512, 128)
+        flat = vel_v.reshape(3, 4, 520, 128)
         wait_all(vel_v.at[:, :, pl.ds(0, 32), pl.ds(0, 2)], vel_recv.at[part])
 
         def product(b, carry):
@@ -397,7 +399,7 @@
         lax.fori_loop(1, 64, send, 0, unroll=7)
 
     def collect(part):
-        wait_all(br.at[part], b_recv.at[part])
+        wait_all(br.at[part, pl.ds(0, 512)], b_recv.at[part])
         for n in range(2):
             v = [br[part, pl.ds(4 * n + i, 64, stride=8), :] for i in range(4)]
             u = regroup(v)
@@ -406,7 +408,7 @@
                 for i in range(4):
                     r_v[pl.ds(8 * c + 4 * n + i, 32, stride=16), :] = turned[i * 32 : i * 32 + 32]
         lanes = pl.ds(part * 128, 128)
-        return acc[...] + dot3(split(r_v[...]), (tbp_hl[0, :, lanes], tbp_hl[1, :, lanes]), LAST)
+        return acc[...] + dot3(split(r_v[pl.ds(0, 512), :]), (tbp_hl[0, :, lanes], tbp_hl[1, :, lanes]), LAST)
 
     for copy in loads[1:6]:
         copy.wait()
@@ -421,13 +423,13 @@
     prepare_divisor()
     gradient_stage(0)
     along_stage(0)
+    span_stage(0, 1)
     gradient_stage(1)
     along_stage(1)
+    span_stage(1, 1)
     prepare_theta()
-    span_stage(0, 1)
     span_back_stage(0)
     span_back_stage(1)
-    span_stage(1, 1)
     gradient_stage(2)
     along_stage(2)
     gradient_stage(3)
@@ -472,11 +474,11 @@
         in_specs=[pl.BlockSpec(memory_space=pl.ANY)] * 12,
         out_specs=pl.BlockSpec(memory_space=pl.ANY),
         scratch_shapes=[
-            blocked, blocked, square, square, square, vm((1, 512), F32), vm((3, 4, 64, 8, 128), F32),
+            vm((4, 528, 128), F32), blocked, square, square, square, vm((1, 512), F32), vm((3, 4, 65, 8, 128), F32),
             table, table, table, table, table, table,
             table, table, table, table, square,
             vm((2, 2, 64, 16, 128), F32),
-            vm((2, 2, 1024, 128), F32),
+            vm((2, 2, 1056, 128), F32),
             vm((2, 512, 128), BF16),
             vm((4, 3, 512, 128), F32),
             vm((4, 3, 512, 128), F32),
@@ -486,9 +488,9 @@
             vm((4, 512, 128), F32),
             vm((4, 512, 128), F32),
             vm((4, 2, 256, 128), F32),
-            vm((4, 512, 128), F32),
+            vm((4, 520, 128), F32),
             table,
-            vm((512, 128), F32),
+            vm((528, 128), F32),
             vm((512, 512), BF16),
             table,
             square,

time: 101 us -> 99.5 us (0.985)
  Pallas kernels: 98.5 us -> 97.1 us
    pallas_call x1, Pallas kernels: 98.5 us -> 97.1 us  [shards(): pl.pallas_call(kernel, out_shape=jax.ShapeDtypeStruct((512, 512), F32), i...]
where the time goes in v3:
time: 99.5 us; the launch traced here: 99.4 us
  Pallas kernels  97.1 us (98%)
  local copies, waits for them, and re-layouts  2.31 us (2%)
    pallas_call x1, Pallas kernels, shards(): pl.pallas_call(kernel, out_shape=jax.ShapeDtypeStruct((512, 512), F32), i...  97.1 us
    unnamed x1, local copies, waits for them, and re-layouts  2.31 us

profile of v3, /device:TPU:1, one launch (start us, length us, event | category | flops | bytes accessed | tf_op | source)
XLA Modules:
  0.0 99.4 jit_solution(5338010353347940850)
XLA Ops:
  0.0 97.1 %shard_map.118 = f32[512,512]{1,0:T(8,128)} custom-call(f32[512,512]{1,0:T(8,128)} %bitcast.4, f32[3,32,16,512]{3,2,1,0:T(8,128)} %velocity.1, f32[512,512]{1,0:T(8,128)} %wall.1, f32[512,512]{1,0:T(8,128)} %to_basis.1, f32[512,512]{1,0:T(8,128)} %from_basis.1, f32[1,512]{1,0:T(1,128)} %bitcast.5, bf16[2,512,512]{2,1,0:T(8,128)(2,1)} %constant.12.clone.span_inv_h, ...), custom_call_target="tpu_custom_call" | custom-call | flops 8000000000 | bytes 16777216 | tf_op jit(solution)/shard_map/pallas_call | solution.py:471
  97.1 2.3 %copy.14 = f32[32,2,8,512]{3,2,1,0:T(8,128)} copy(f32[32,2,8,512]{3,2,1,0:T(8,128)} %bitcast.3) | data formatting | bytes 2097152

commit v4 on v3

--- a/solution.py
+++ b/solution.py
@@ -274,21 +274,25 @@
     def span_stage(f, c):
         wait_all(fr.at[f, c, pl.ds(0, 1024)], f_recv.at[f, c])
 
-        def sub(i, carry):
-            part = 2 * c + i
-
-            def collect_modes(t, carry):
-                start = (t % 2) * 8 + (t // 2) * 4 + 2 * i
-                v = [fr[f, c, pl.ds(start + 16 * yl + j, 32, stride=32), :] for yl in range(2) for j in range(2)]
+        def collect_modes(t, carry):
+            start = lax.rem(t, 2) * 8 + lax.div(t, 2) * 4
+            for i in range(2):
+                v = [
+                    fr[f, c, pl.ds(start + 2 * i + 16 * yl + j, 32, stride=32), :] for yl in range(2) for j in range(2)
+                ]
+                lanes = pl.ds(i * 128, 128)
                 for n, u in enumerate(regroup(v)):
                     rows = pl.ds(pl.multiple_of(t * 128 + n * 32, 32), 32)
-                    x_hl[0, rows, :], x_hl[1, rows, :] = split(u)
-                return carry
-
-            lax.fori_loop(0, 4, collect_modes, 0)
-            for table, h in ((span_inv, 0), (span_der, 1)) if f == 0 else ((span_inv, 2),):
-                xs[part, h] = dot3((table[0], table[1]), (x_hl[0], x_hl[1]))
-                mine = pl.ds(pl.multiple_of(mx * 128, 128), 128)
+                    x_hl[0, rows, lanes], x_hl[1, rows, lanes] = split(u)
+            return carry
+
+        lax.fori_loop(0, 4, collect_modes, 0)
+        mine = pl.ds(pl.multiple_of(mx * 128, 128), 128)
+        for table, h in ((span_inv, 0), (span_der, 1)) if f == 0 else ((span_inv, 2),):
+            value = dot3((table[0], table[1]), (x_hl[0], x_hl[1]))
+            for i in range(2):
+                xs[2 * c + i, h] = value[:, i * 128 : i * 128 + 128]
+            for part in (2 * c, 2 * c + 1):
 
                 def send(k, carry):
                     other = wrap(mx + k, 4)
@@ -304,9 +308,6 @@
 
                 lax.fori_loop(1, 4, send, 0)
                 pltpu.make_async_copy(xs.at[part, h, mine], xr.at[part, h, mine], x_recv.at[part, h]).start()
-            return carry
-
-        lax.fori_loop(0, 2, sub, 0)
 
     def gradient_stage(part):
         def gather_lines(n, carry):
@@ -479,7 +480,7 @@
             table, table, table, table, square,
             vm((2, 2, 64, 16, 128), F32),
             vm((2, 2, 1056, 128), F32),
-            vm((2, 512, 128), BF16),
+            vm((2, 512, 256), BF16),
             vm((4, 3, 512, 128), F32),
             vm((4, 3, 512, 128), F32),
             vm((3, 2, 128, 512), BF16),

time: 99.5 us -> 102 us (1.025)
  Pallas kernels: 97.1 us -> 99.2 us
    pallas_call x1, Pallas kernels: 97.1 us -> 99.2 us  [shards(): pl.pallas_call(kernel, out_shape=jax.ShapeDtypeStruct((512, 512), F32), i...]
where the time goes in v4:
time: 102 us
  Pallas kernels  99.2 us (97%)
  local copies, waits for them, and re-layouts  2.31 us (2%)
    pallas_call x1, Pallas kernels, shards(): pl.pallas_call(kernel, out_shape=jax.ShapeDtypeStruct((512, 512), F32), i...  99.2 us
    unnamed x1, local copies, waits for them, and re-layouts  2.31 us

profile of v4, /device:TPU:1, one launch (start us, length us, event | category | flops | bytes accessed | tf_op | source)
XLA Modules:
  0.0 101.5 jit_solution(9770287848424069564)
XLA Ops:
  0.0 99.2 %shard_map.118 = f32[512,512]{1,0:T(8,128)} custom-call(f32[512,512]{1,0:T(8,128)} %bitcast.4, f32[3,32,16,512]{3,2,1,0:T(8,128)} %velocity.1, f32[512,512]{1,0:T(8,128)} %wall.1, f32[512,512]{1,0:T(8,128)} %to_basis.1, f32[512,512]{1,0:T(8,128)} %from_basis.1, f32[1,512]{1,0:T(1,128)} %bitcast.5, bf16[2,512,512]{2,1,0:T(8,128)(2,1)} %constant.12.clone.span_inv_h, ...), custom_call_target="tpu_custom_call" | custom-call | flops 8000000000 | bytes 16777216 | tf_op jit(solution)/shard_map/pallas_call | solution.py:472
  99.2 2.3 %copy.14 = f32[32,2,8,512]{3,2,1,0:T(8,128)} copy(f32[32,2,8,512]{3,2,1,0:T(8,128)} %bitcast.3) | data formatting | bytes 2097152
